TPU v7x, 256 devices: a whole 4x4x8 slice. The times are simulated.
256 devices in a mesh: slab: 8 (over z), col: 32 (over x, y, core).
Axes of the slice: x: 4, y: 4, z: 8, core: 2. Of those that a mesh axis runs over, the one named last changes fastest.
Arguments:
- tensor: float32 [128, 2048, 2048], P('slab', 'col')
- signs3: int32 [2048], replicated, may hold values from -1 to 1, as said below
- picked3: int32 [256], replicated, may hold values from 0 to 2047, as said below
- signs2: int32 [2048], replicated, may hold values from -1 to 1, as said below
- picked2: int32 [256], replicated, may hold values from 0 to 2047, as said below
Outputs:
- basis: float32 [256, 128, 256], P('col', 'slab')
Inputs may be any that keep to these rules, and one draw needn't show every extreme that they name: `signs3`: each entry is -1 or 1. `signs2`: each entry is -1 or 1. `picked3`: distinct and increasing; 0 and 2047 are always among them. `picked2`: distinct and increasing; 0 and 2047 are always among them.
All inputs are finite; a program needn't handle non-finite values.
Results may differ from a plain program's by a relative error of at most 0.0003.
Values sent between devices are 32-bit elements; how exact they have to be, the bound alone decides.
A program may use at most 64 MiB of HBM per device.

v0:
```python
import jax
import jax.numpy as jnp
from jax import lax
from jax.sharding import PartitionSpec as P


def hadamard_rows(picked, columns, bits):
    parity = jnp.zeros((picked.shape[0], columns.shape[0]), jnp.int32)
    for place in range(bits):
        upper = jnp.bitwise_and(jnp.right_shift(picked, place), 1)
        lower = jnp.bitwise_and(jnp.right_shift(columns, place), 1)
        parity = parity + upper[:, None] * lower[None, :]
    return (1 - 2 * (parity % 2)).astype(jnp.float32)


def invert_lower(gram):
    lower = jnp.linalg.cholesky(gram)
    identity = jnp.eye(gram.shape[0], dtype=jnp.float32)
    return lax.linalg.triangular_solve(lower, identity, left_side=True, lower=True)


def on_device(tensor, signs3, picked3, signs2, picked2):
    rows, width, length = tensor.shape
    col_count = lax.axis_size("col")
    rank_two = picked2.shape[0]
    rank_three = picked3.shape[0]
    full_width = signs2.shape[0]
    share = rank_two // col_count
    scale = jnp.float32((rank_two * rank_three) ** 0.5)
    highest = lax.Precision.HIGHEST
    width_bits = full_width.bit_length() - 1
    table3 = hadamard_rows(picked3, jnp.arange(length, dtype=jnp.int32), length.bit_length() - 1)
    table3 = table3 * signs3.astype(jnp.float32)[None, :]
    first = jnp.dot(
        tensor.reshape(rows * width, length),
        table3.T,
        precision=highest,
        preferred_element_type=jnp.float32,
    )
    first = first.reshape(rows, width, rank_three)
    start = lax.axis_index("col") * width
    columns = start + jnp.arange(width, dtype=jnp.int32)
    own_signs = lax.dynamic_slice_in_dim(signs2, start, width, 0)
    table2 = hadamard_rows(picked2, columns, width_bits)
    table2 = table2 * own_signs.astype(jnp.float32)[None, :]
    whole = lax.psum(
        jnp.einsum(
            "rj,ijk->rik", table2, first, precision=highest, preferred_element_type=jnp.float32
        ),
        "col",
    )
    own = lax.dynamic_slice_in_dim(whole, lax.axis_index("col") * share, share, 0)
    gathered = lax.all_gather(own, "slab", axis=1, tiled=True)
    partial_value = jnp.einsum(
        "rik,rjk->ij", gathered, gathered, precision=highest, preferred_element_type=jnp.float32
    )
    gram = lax.psum(partial_value, "col")
    inverse = invert_lower(gram)
    mine = lax.dynamic_slice_in_dim(inverse, lax.axis_index("slab") * rows, rows, 0)
    basis = jnp.einsum(
        "ik,rkc->ric", mine, gathered, precision=highest, preferred_element_type=jnp.float32
    )
    return basis * scale


def solution(mesh):
    placed = (P("slab", "col", None), P(), P(), P(), P())
    return jax.shard_map(
        on_device, mesh=mesh, in_specs=placed, out_specs=P("col", "slab", None), check_vma=False
    )
```

profile of v0, /device:TPU:1, one launch (start us, length us, event | category | flops | bytes accessed | tf_op | source)
XLA Modules:
  0.0 335.7 jit_solution(9460332460749227021)
XLA Ops:
  6.5 0.0 all-reduce.3.cloned.1.call-start
  6.7 0.7 convert_element_type.16
  7.4 0.7 shift-right-arithmetic_and_fusion.21
  8.0 0.7 shift-right-arithmetic_and_fusion.32
  8.7 13.0 %fusion.10 = f32[1024,256]{0,1:T(8,128)S(1)} fusion(f32[1024,2048]{1,0:T(8,128)} %bitcast.26, f32[2048]{0:T(1024)S(1)} %convert_element_type.16, s32[2048]{0:T(1024)S(1)} %get-tuple-element.27, s32[256]{0:T(256)S(1)} %get-tuple-element.25, s32[2048]{0:T(1024)S(1)} %get-tuple-element.28, s32[256]{0:T(256)S(1)} %get-tuple-element.26, ...), kind=kOutput, calls=%fused_computation.12 | convolution fusion | flops 6461325312 | bytes 9546752 | tf_op jit(solution)/shard_map/dot_general | solution.py:34
  21.7 0.3 copy.18
  22.1 0.8 dynamic-slice_convert_fusion
  22.9 5.4 %fusion.49 = f32[256,16,256]{2,0,1:T(8,128)} fusion(f32[16,64,256]{2,1,0:T(8,128)S(1)} %bitcast.25, f32[64]{0:T(128)S(1)} %get-tuple-element.47, s32[64]{0:T(128)S(1)} %get-tuple-element.37, s32[256]{0:T(256)S(1)} %get-tuple-element.14, s32[64]{0:T(128)S(1)} %get-tuple-element.38, s32[256]{0:T(256)S(1)} %get-tuple-element.15, s32[64]{0:T(128)S(1)} %get-tuple-element.39, ...), kind=kOutput, calls=%fused_computation.55 | convolution fusion | flops 805896192 | bytes 5257216 | tf_op jit(solution)/shard_map/rj,ijk->rik/dot_general | solution.py:47
  28.3 0.0 all-reduce.3.cloned.1.call-update
  28.3 0.2 all-gather.2.cloned.1.call-start
  28.5 125.5 %all-reduce.3.cloned.1.call-done = f32[256,16,256]{2,0,1:T(8,128)} async-done(((f32[256,16,256]{2,0,1:T(8,128)}), f32[256,16,256]{2,0,1:T(8,128)}) %all-reduce.3.cloned.1.call-update) | async-done | bytes 4194320 | tf_op jit(solution)/shard_map/psum | solution.py:46
  154.0 1.6 constant_dynamic-slice_fusion
  155.6 0.0 all-gather.2.cloned.1.call-update
  155.6 0.0 all-reduce.5.cloned.1.call-start
  155.6 33.5 %all-gather.2.cloned.1.call-done = f32[8,128,256]{2,0,1:T(8,128)} async-done(((f32[8,16,256]{2,0,1:T(8,128)}), f32[8,128,256]{2,0,1:T(8,128)}) %all-gather.2.cloned.1.call-update) | async-done | bytes 1048592 | tf_op jit(solution)/shard_map/all_gather | solution.py:53
  189.1 0.0 copy-start
  189.1 3.8 %convolution_bitcast_fusion = f32[128,128]{0,1:T(8,128)} fusion(f32[8,128,256]{2,0,1:T(8,128)} %all-gather.2.cloned.1.call-done), kind=kOutput, calls=%fused_computation.15 | convolution fusion | flops 402653184 | bytes 1114112 | tf_op jit(solution)/shard_map/rik,rjk->ij/dot_general | solution.py:54
  192.9 0.0 all-reduce.5.cloned.1.call-update
  192.9 109.7 %all-reduce.5.cloned.1.call-done = f32[128,128]{0,1:T(8,128)} async-done(((f32[128,128]{0,1:T(8,128)}), f32[128,128]{0,1:T(8,128)}) %all-reduce.5.cloned.1.call-update) | async-done | bytes 65552 | tf_op jit(solution)/shard_map/psum | solution.py:57
  302.6 0.9 copy.22
  303.6 0.9 fusion.53
  304.4 11.7 %cholesky.17 = f32[128,128]{1,0:T(8,128)S(1)} custom-call(f32[128,128]{1,0:T(8,128)S(1)} %fusion.53), custom_call_target="Cholesky" | custom-call | tf_op jit(solution)/shard_map/jit(cholesky)/cholesky | solution.py:17
  316.2 0.6 compare_reduce_fusion
  316.8 0.7 fusion.42
  317.5 9.8 %custom-call.6 = f32[1,128,128]{1,2,0:T(8,128)S(1)} custom-call(f32[1,128,128]{2,1,0:T(8,128)S(1)} %fusion.42), custom_call_target="InvertDiagBlocksLowerTriangular" | custom-call | tf_op jit(solution)/shard_map/triangular_solve | solution.py:19
  327.3 0.2 fusion.51
  327.6 0.0 copy-done
  327.6 1.6 fusion.13
  (12 shorter events, 0.1 us)
Async XLA Ops:
  6.5 147.5 %all-reduce.3.cloned.1.call-start = ((), (), s32[]{:S(2)}) async-start(), calls=%async_computation | async-start | bytes 8388608 | tf_op jit(solution)/shard_map/psum | solution.py:46
  28.3 160.9 %all-gather.2.cloned.1.call-start = ((), (), s32[]{:S(2)}) async-start(), calls=%async_computation.1 | async-start | bytes 1179648 | tf_op jit(solution)/shard_map/all_gather | solution.py:53
  155.6 147.1 %all-reduce.5.cloned.1.call-start = ((), (), s32[]{:S(2)}) async-start(), calls=%async_computation.2 | async-start | bytes 131072 | tf_op jit(solution)/shard_map/psum | solution.py:57
  189.1 138.4 %copy-start = (f32[8,128,256]{2,0,1:T(8,128)S(1)}, f32[8,128,256]{2,0,1:T(8,128)}, u32[]{:S(2)}) copy-start(f32[8,128,256]{2,0,1:T(8,128)} %all-gather.2.cloned.1.call-done) | copy-start | bytes 3145732
Sparse Core Ops, SparseCore 0:
  28.4 125.5 all-reduce.2
  155.8 33.3 all-gather.1
  193.0 109.5 all-reduce.4
where the time goes:
time: 336 us
  waiting for transfers between devices  269 us (80%)
  other arithmetic  26.6 us (8%)
  matrix products  24 us (7%)
  between operations  13.2 us (4%)
    psum x1, waiting for transfers between devices, on_device(): lax.psum(jnp.einsum('rj,ijk->rik', table2, first, precision=highest, pref...  125 us
    psum x1, waiting for transfers between devices, on_device(): gram = lax.psum(partial_value, 'col')  110 us
    all_gather x1, waiting for transfers between devices, on_device(): gathered = lax.all_gather(own, 'slab', axis=1, tiled=True)  33.5 us
    dot_general x1, matrix products, on_device(): jnp.dot(tensor.reshape(rows * width, length), table3.T, precision=highest...  13 us
    another operation x3, other arithmetic, invert_lower(): lower = jnp.linalg.cholesky(gram)  12.4 us
    another operation x2, other arithmetic, invert_lower(): lax.linalg.triangular_solve(lower, identity, left_side=True, lower=True)  10.5 us
  transfers between devices with their start and end apart: 3, of which 3 were waited for; matrix products, arithmetic and copies ran while one was open for 0% of the time, Pallas kernels for 0%

commit v1 on v0

v1 whole, which is shorter than its diff:
```python
import jax
import jax.numpy as jnp
from jax import lax
from jax.experimental import pallas as pl
from jax.experimental.pallas import tpu as pltpu
from jax.sharding import PartitionSpec as P

MESH = pl.DeviceIdType.MESH
SIDE = 4
CHIPS = SIDE * SIDE
CORES = 2
COLS = CHIPS * CORES
SLABS = 8
WIDTH = 64
LENGTH = 2048
RANK = 256
HALF = 128
ROWS = SLABS * CHIPS
BLOCK = 8
F32 = jnp.float32
BF16 = jnp.bfloat16


def split_two(value):
    high = value.astype(BF16)
    return high, (value - high.astype(F32)).astype(BF16)


def split_three(value):
    high = value.astype(BF16)
    rest = value - high.astype(F32)
    middle = rest.astype(BF16)
    return high, middle, (rest - middle.astype(F32)).astype(BF16)


def exact_dot(left, right, dims):
    lh, lm, ll = split_three(left)
    rh, rm, rl = split_three(right)
    (la,), (ra,) = dims
    return lax.dot_general(
        jnp.concatenate([lh, lh, lm, lm, lh, ll], axis=la),
        jnp.concatenate([rh, rm, rh, rm, rl, rh], axis=ra),
        (dims, ((), ())),
        preferred_element_type=F32,
    )


def odd(value):
    value = value ^ (value >> 8)
    value = value ^ (value >> 4)
    value = value ^ (value >> 2)
    value = value ^ (value >> 1)
    return (1 - 2 * (value & 1)).astype(F32)


def inverse_factor(held):
    lane = lax.broadcasted_iota(jnp.int32, (BLOCK, ROWS), 1)
    sub = lax.broadcasted_iota(jnp.int32, (BLOCK, ROWS), 0)
    for base in range(0, ROWS, BLOCK):
        rows = [
            jnp.broadcast_to(held[base + i : base + i + 1, :], (BLOCK, ROWS)) for i in range(BLOCK)
        ]
        cell = {}
        for i in range(BLOCK):
            for j in range(i + 1):
                cell[i, j] = jnp.broadcast_to(rows[i][:, base + j : base + j + 1], (BLOCK, ROWS))
        own = jnp.logical_and(lane >= base, lane < base + BLOCK)
        rows = [
            jnp.where(own, jnp.where(lane == base + i, F32(1), F32(0)), rows[i])
            for i in range(BLOCK)
        ]
        for k in range(BLOCK):
            root = lax.rsqrt(cell[k, k])
            rows[k] = rows[k] * root
            for i in range(k + 1, BLOCK):
                cell[i, k] = cell[i, k] * root
            for i in range(k + 1, BLOCK):
                for j in range(k + 1, i + 1):
                    cell[i, j] = cell[i, j] - cell[i, k] * cell[j, k]
                rows[i] = rows[i] - cell[i, k] * rows[k]
        tile = rows[0]
        for i in range(1, BLOCK):
            tile = jnp.where(sub == i, rows[i], tile)
        held[base : base + BLOCK, :] = tile
        if base + BLOCK < ROWS:
            update = exact_dot(tile, tile, ((0,), (0,)))
            rest = held[base + BLOCK :, :]
            clear = lax.broadcasted_iota(jnp.int32, rest.shape, 1)
            clear = jnp.logical_and(clear >= base, clear < base + BLOCK)
            held[base + BLOCK :, :] = jnp.where(clear, F32(0), rest) - update[base + BLOCK :, :]


def kernel(
    tensor, signs3, picked3, signs2, picked2, out,
    slabs, table3, table2, outgoing, landed, sketch, spread, slices, planes,
    partial_gram, terms, row_block, blocks, block, gram, result, returned,
    load_sem, send_sem, recv_sem, spread_send, spread_recv, slice_send, slice_recv,
    term_send, term_recv, block_send, block_recv, gram_send, gram_recv, back_send, back_recv,
):
    z = lax.axis_index("slab")
    p = lax.axis_index("col")
    q = p // CORES
    h = p % CORES
    x, y = q // SIDE, q % SIDE

    def shifted(step, sign):
        turn = (step + 1) % CHIPS
        dx, dy = turn // SIDE, turn % SIDE
        return ((x + sign * dx + SIDE) % SIDE) * SIDE + (y + sign * dy + SIDE) % SIDE

    def load(step):
        return pltpu.make_async_copy(tensor.at[shifted(step, 1)], slabs.at[step], load_sem.at[step])

    @pl.loop(0, CHIPS)
    def _(step):
        load(step).start()

    barrier = pltpu.get_barrier_semaphore()

    @pl.loop(1, COLS)
    def _(step):
        pl.semaphore_signal(barrier, 1, device_id=(z, (p + step) % COLS), device_id_type=MESH)

    @pl.loop(1, SLABS)
    def _(step):
        for core in range(CORES):
            pl.semaphore_signal(
                barrier, 1, device_id=((z + step) % SLABS, q * CORES + core), device_id_type=MESH
            )

    below = lax.broadcasted_iota(jnp.int32, (HALF, HALF), 0)
    for half in range(RANK // HALF):
        picks = picked3[half : half + 1, :]
        low = odd(below & jnp.broadcast_to(picks, (HALF, HALF)))
        for tile in range(LENGTH // HALF):
            high = odd(jnp.broadcast_to(picks, (BLOCK, HALF)) & (tile * HALF))[:1]
            table3[tile * HALF : (tile + 1) * HALF, half * HALF : (half + 1) * HALF] = (
                low * high
            ).astype(BF16)
    along = lax.broadcasted_iota(jnp.int32, (HALF, HALF), 1)
    for half in range(RANK // HALF):
        picks = picked2[half : half + 1, :].astype(F32)
        picks = jnp.broadcast_to(picks, (HALF, HALF)).T.astype(jnp.int32)
        low = odd(along & picks)
        for tile in range(CHIPS):
            high = odd(picks & (tile * HALF))
            signs = signs2[tile : tile + 1, :].astype(F32)
            table2[tile, half * HALF : (half + 1) * HALF, :] = (low * high * signs).astype(BF16)

    pl.semaphore_wait(barrier, COLS - 1 + (SLABS - 1) * CORES)

    def piece(step, core):
        chip = shifted(step, 1)
        return pltpu.make_async_remote_copy(
            outgoing.at[step, core],
            landed.at[p],
            send_sem.at[step, core],
            recv_sem.at[p],
            device_id=(z, chip * CORES + core),
            device_id_type=MESH,
        )

    @pl.loop(0, CHIPS, step=2)
    def _(step):
        load(step).wait()
        load(step + 1).wait()
        both = slabs[pl.ds(step, 2)].reshape(2 * WIDTH, LENGTH)
        highs, lows = [], []
        for tile in range(LENGTH // HALF):
            signs = signs3[tile : tile + 1, :].astype(F32)
            high, low = split_two(both[:, tile * HALF : (tile + 1) * HALF] * signs)
            highs.append(high)
            lows.append(low)
        left = jnp.concatenate(
            [jnp.concatenate(highs, axis=1), jnp.concatenate(lows, axis=1)], axis=0
        )
        first = jnp.dot(left, table3[...], preferred_element_type=F32)
        first = first[: 2 * WIDTH] + first[2 * WIDTH :]
        for part in range(2):
            for core in range(CORES):
                outgoing[step + part, core] = first[
                    part * WIDTH : (part + 1) * WIDTH, core * HALF : (core + 1) * HALF
                ]
        for core in range(CORES):
            piece(step, core).start()

        @pl.when(step + 1 < CHIPS - 1)
        def _():
            for core in range(CORES):
                piece(step + 1, core).start()

        @pl.when(step + 1 == CHIPS - 1)
        def _():
            piece(step + 1, 1 - h).start()

    landed[p] = outgoing[CHIPS - 1, h]

    def arrival(source):
        return pltpu.make_async_remote_copy(
            outgoing.at[0, 0],
            landed.at[source],
            send_sem.at[0, 0],
            recv_sem.at[source],
            device_id=(z, p ^ 1),
            device_id_type=MESH,
        )

    def two_chips(step, total):
        lefts, rights = [], []
        for part in range(2):
            chip = shifted(step + part, -1)

            @pl.when(step + part < CHIPS - 1)
            def _():
                for core in range(CORES):
                    arrival(chip * CORES + core).wait_recv()

            @pl.when(step + part == CHIPS - 1)
            def _():
                arrival(p ^ 1).wait_recv()

            lefts.append(table2[chip])
            value = landed[pl.ds(chip * CORES, CORES)].reshape(CORES * WIDTH, HALF)
            rights.append(jnp.concatenate(split_two(value), axis=1))
        return total + jnp.dot(
            jnp.concatenate(lefts, axis=1),
            jnp.concatenate(rights, axis=0),
            preferred_element_type=F32,
        )

    total = lax.fori_loop(
        0, CHIPS // 2, lambda n, t: two_chips(2 * n, t), jnp.zeros((RANK, 2 * HALF), F32)
    )
    sketch[...] = (total[:, :HALF] + total[:, HALF:]).reshape(COLS, RANK // COLS, HALF)

    def row_copy(step):
        to = (p + step) % COLS
        return pltpu.make_async_remote_copy(
            sketch.at[to],
            spread.at[q, h],
            spread_send.at[step],
            spread_recv.at[p],
            device_id=(z, to),
            device_id_type=MESH,
        )

    def row_arrival(step):
        source = (p + step) % COLS
        return pltpu.make_async_remote_copy(
            sketch.at[source],
            spread.at[source // CORES, source % CORES],
            spread_send.at[step],
            spread_recv.at[source],
            device_id=(z, source),
            device_id_type=MESH,
        )

    @pl.loop(1, COLS)
    def _(step):
        row_copy(step).start()

    spread[q, h] = sketch[p]

    @pl.loop(1, COLS)
    def _(step):
        row_arrival(step).wait_recv()

    for core in range(CORES):
        for r in range(SLABS):
            slices[r, :, core * HALF : (core + 1) * HALF] = spread[:, core, r, :]

    def slice_copy(step):
        to = (z + step) % SLABS
        return pltpu.make_async_remote_copy(
            slices.at[to],
            planes.at[z],
            slice_send.at[step],
            slice_recv.at[z],
            device_id=(to, p),
            device_id_type=MESH,
        )

    def slice_arrival(step):
        source = (z + step) % SLABS
        return pltpu.make_async_remote_copy(
            slices.at[source],
            planes.at[source],
            slice_send.at[step],
            slice_recv.at[source],
            device_id=(source, p),
            device_id_type=MESH,
        )

    @pl.loop(1, SLABS)
    def _(step):
        slice_copy(step).start()

    planes[z] = slices[z]

    @pl.loop(1, SLABS)
    def _(step):
        slice_arrival(step).wait_recv()

    flat = planes[...].reshape(ROWS, RANK)
    partial_gram[...] = exact_dot(flat, flat, ((1,), (1,))).reshape(CHIPS, BLOCK, ROWS)

    def term_copy(step):
        to = (q + step) % CHIPS
        return pltpu.make_async_remote_copy(
            partial_gram.at[to],
            terms.at[q],
            term_send.at[step],
            term_recv.at[q],
            device_id=(z, to * CORES + h),
            device_id_type=MESH,
        )

    def term_arrival(step):
        source = (q + step) % CHIPS
        return pltpu.make_async_remote_copy(
            partial_gram.at[source],
            terms.at[source],
            term_send.at[step],
            term_recv.at[source],
            device_id=(z, source * CORES + h),
            device_id_type=MESH,
        )

    @pl.loop(1, CHIPS)
    def _(step):
        term_copy(step).start()

    terms[q] = partial_gram[q]

    @pl.loop(1, CHIPS)
    def _(step):
        term_arrival(step).wait_recv()

    row_block[...] = jnp.sum(terms[...], axis=0)

    place = z * CORES + h
    places = SLABS * CORES

    def block_copy(step):
        to = (place + step) % places
        return pltpu.make_async_remote_copy(
            row_block,
            blocks.at[place],
            block_send.at[step],
            block_recv.at[place],
            device_id=(to // CORES, q * CORES + to % CORES),
            device_id_type=MESH,
        )

    def block_arrival(step):
        source = (place + step) % places
        return pltpu.make_async_remote_copy(
            row_block,
            blocks.at[source],
            block_send.at[step],
            block_recv.at[source],
            device_id=(source // CORES, q * CORES + source % CORES),
            device_id_type=MESH,
        )

    @pl.loop(1, places)
    def _(step):
        block_copy(step).start()

    blocks[place] = row_block[...]

    @pl.loop(1, places)
    def _(step):
        block_arrival(step).wait_recv()

    block[...] = jnp.sum(blocks[...], axis=0)

    def gram_copy(step):
        to = (q + step) % CHIPS
        return pltpu.make_async_remote_copy(
            block,
            gram.at[pl.ds(q * BLOCK, BLOCK)],
            gram_send.at[step],
            gram_recv.at[q],
            device_id=(z, to * CORES + h),
            device_id_type=MESH,
        )

    def gram_arrival(step):
        source = (q + step) % CHIPS
        return pltpu.make_async_remote_copy(
            block,
            gram.at[pl.ds(source * BLOCK, BLOCK)],
            gram_send.at[step],
            gram_recv.at[source],
            device_id=(z, source * CORES + h),
            device_id_type=MESH,
        )

    @pl.loop(1, CHIPS)
    def _(step):
        gram_copy(step).start()

    gram[pl.ds(pl.multiple_of(q * BLOCK, BLOCK), BLOCK), :] = block[...]

    @pl.loop(1, CHIPS)
    def _(step):
        gram_arrival(step).wait_recv()

    inverse_factor(gram)

    row = lax.broadcasted_iota(jnp.int32, (ROWS, ROWS), 0)
    col = lax.broadcasted_iota(jnp.int32, (ROWS, ROWS), 1)
    inverse = jnp.where(col <= row, gram[...], F32(0)) * F32(RANK)
    result[...] = exact_dot(inverse, flat, ((1,), (0,))).reshape(SLABS, CHIPS, RANK)

    def back_copy(step):
        to = (z + step) % SLABS
        return pltpu.make_async_remote_copy(
            result.at[to],
            returned.at[z],
            back_send.at[step],
            back_recv.at[z],
            device_id=(to, p),
            device_id_type=MESH,
        )

    def back_arrival(step):
        source = (z + step) % SLABS
        return pltpu.make_async_remote_copy(
            result.at[source],
            returned.at[source],
            back_send.at[step],
            back_recv.at[source],
            device_id=(source, p),
            device_id_type=MESH,
        )

    @pl.loop(1, SLABS)
    def _(step):
        back_copy(step).start()

    out[z] = result[z]

    @pl.loop(1, SLABS)
    def _(step):
        back_arrival(step).wait_recv()
        source = (z + step) % SLABS
        out[source] = returned[source]

    @pl.loop(0, CHIPS - 1)
    def _(step):
        for core in range(CORES):
            piece(step, core).wait_send()

    piece(CHIPS - 1, 1 - h).wait_send()

    @pl.loop(1, COLS)
    def _(step):
        row_copy(step).wait_send()

    @pl.loop(1, SLABS)
    def _(step):
        slice_copy(step).wait_send()
        back_copy(step).wait_send()

    @pl.loop(1, CHIPS)
    def _(step):
        term_copy(step).wait_send()
        block_copy(step).wait_send()
        gram_copy(step).wait_send()


def on_device(tensor, signs3, picked3, signs2, picked2):
    vmem = pl.BlockSpec(memory_space=pltpu.VMEM)
    dma = pltpu.SemaphoreType.DMA
    places = SLABS * CORES
    return pl.pallas_call(
        kernel,
        out_shape=jax.ShapeDtypeStruct((RANK // COLS, CHIPS, RANK), F32),
        in_specs=[pl.BlockSpec(memory_space=pl.ANY)] + [vmem] * 4,
        out_specs=vmem,
        scratch_shapes=[
            pltpu.VMEM((CHIPS, WIDTH, LENGTH), F32),
            pltpu.VMEM((LENGTH, RANK), BF16),
            pltpu.VMEM((CHIPS, RANK, HALF), BF16),
            pltpu.VMEM((CHIPS, CORES, WIDTH, HALF), F32),
            pltpu.VMEM((COLS, WIDTH, HALF), F32),
            pltpu.VMEM((COLS, RANK // COLS, HALF), F32),
            pltpu.VMEM((CHIPS, CORES, RANK // COLS, HALF), F32),
            pltpu.VMEM((SLABS, CHIPS, RANK), F32),
            pltpu.VMEM((SLABS, CHIPS, RANK), F32),
            pltpu.VMEM((CHIPS, BLOCK, ROWS), F32),
            pltpu.VMEM((CHIPS, BLOCK, ROWS), F32),
            pltpu.VMEM((BLOCK, ROWS), F32),
            pltpu.VMEM((places, BLOCK, ROWS), F32),
            pltpu.VMEM((BLOCK, ROWS), F32),
            pltpu.VMEM((ROWS, ROWS), F32),
            pltpu.VMEM((SLABS, CHIPS, RANK), F32),
            pltpu.VMEM((SLABS, CHIPS, RANK), F32),
            dma((CHIPS,)),
            dma((CHIPS, CORES)),
            dma((COLS,)),
            dma((COLS,)),
            dma((COLS,)),
            dma((SLABS,)),
            dma((SLABS,)),
            dma((CHIPS,)),
            dma((CHIPS,)),
            dma((places,)),
            dma((places,)),
            dma((CHIPS,)),
            dma((CHIPS,)),
            dma((SLABS,)),
            dma((SLABS,)),
        ],
        compiler_params=pltpu.CompilerParams(
            collective_id=0, has_side_effects=True, vmem_limit_bytes=40 * 1024 * 1024
        ),
        name="sketch_basis",
    )(
        tensor,
        signs3.reshape(LENGTH // HALF, HALF),
        picked3.reshape(RANK // HALF, HALF),
        signs2.reshape(CHIPS, HALF),
        picked2.reshape(RANK // HALF, HALF),
    )


def solution(mesh):
    placed = (P("slab", "col", None), P(), P(), P(), P())
    return jax.shard_map(
        on_device, mesh=mesh, in_specs=placed, out_specs=P("col", "slab", None), check_vma=False
    )
```

time: 336 us -> 77.5 us (0.23)
  waiting for transfers between devices: 269 us -> 0 us
  Pallas kernels: 0 us -> 70.3 us
  other arithmetic: 26.6 us -> 0 us
  matrix products: 24 us -> 0 us
  between operations: 13.2 us -> 0.01 us
  local copies, waits for them, and re-layouts: 2.83 us -> 6.79 us
    psum x2 -> x0, waiting for transfers between devices: 235 us -> none  [the longest x1 125 us: on_device(): lax.psum(jnp.einsum('rj,ijk->rik', table2, first, precision=highest, pref...]
    pallas_call x0 -> x1, Pallas kernels: none -> 70.3 us  [on_device(): pl.pallas_call(kernel, out_shape=jax.ShapeDtypeStruct((RANK // COLS, CHIP...]
    all_gather x1 -> x0, waiting for transfers between devices: 33.5 us -> none  [on_device(): gathered = lax.all_gather(own, 'slab', axis=1, tiled=True)]
    dot_general x4 -> x0, matrix products: 23.8 us -> none  [the longest x1 13 us: on_device(): jnp.dot(tensor.reshape(rows * width, length), table3.T, precision=highest...]
    another operation x5 -> x0, other arithmetic: 22.9 us -> none  [the longest x3 12.4 us: invert_lower(): lower = jnp.linalg.cholesky(gram)]
    unnamed x2 -> x11, local copies, waits for them, and re-layouts: 0.01 us -> 6.79 us
  transfers between devices with their start and end apart: 3 -> 0, of which waited for: 3 -> 0; matrix products, arithmetic and copies ran while one was open for 0% -> 0% of each run, Pallas kernels for 0% -> 0%
where the time goes in v1:
time: 77.5 us; the launch traced here: 77.1 us
  Pallas kernels  70.3 us (91%)
  local copies, waits for them, and re-layouts  6.79 us (9%)
    pallas_call x1, Pallas kernels, on_device(): pl.pallas_call(kernel, out_shape=jax.ShapeDtypeStruct((RANK // COLS, CHIP...  70.3 us
    unnamed x11, local copies, waits for them, and re-layouts  6.79 us

profile of v1, /device:TPU:1, one launch (start us, length us, event | category | flops | bytes accessed | tf_op | source)
XLA Modules:
  0.0 77.1 jit_solution(1975394658825434418)
XLA Ops:
  0.0 0.0 copy-start
  0.0 3.4 %copy-done = f32[16,64,2048]{2,1,0:T(8,128)S(1)} copy-done((f32[16,64,2048]{2,1,0:T(8,128)S(1)}, f32[16,64,2048]{2,1,0:T(8,128)}, u32[]{:S(2)}) %copy-start) | copy-done | bytes 8388632
  3.4 0.0 copy-start.1
  3.4 0.7 copy-done.1
  4.1 0.0 copy-start.2
  4.1 0.7 copy-done.2
  4.8 0.0 copy-start.3
  4.8 0.7 copy-done.3
  5.5 0.0 copy-start.4
  5.5 0.7 copy-done.4
  6.1 70.3 %sketch_basis.1 = f32[8,16,256]{2,1,0:T(8,128)S(1)} custom-call(f32[16,64,2048]{2,1,0:T(8,128)S(1)} %copy-done, s32[16,128]{1,0:T(8,128)S(1)} %bitcast.4, s32[2,128]{1,0:T(2,128)S(1)} %bitcast.6, s32[16,128]{1,0:T(8,128)S(1)} %bitcast.5, s32[2,128]{1,0:T(2,128)S(1)} %bitcast.7), custom_call_target="tpu_custom_call" | custom-call | tf_op jit(solution)/shard_map/sketch_basis/pallas_call | solution.py:478
  76.5 0.7 copy.7
Async XLA Ops:
  0.0 3.4 %copy-start = (f32[16,64,2048]{2,1,0:T(8,128)S(1)}, f32[16,64,2048]{2,1,0:T(8,128)}, u32[]{:S(2)}) copy-start(f32[16,64,2048]{2,1,0:T(8,128)} %tensor.1) | copy-start | bytes 25165828
  3.4 0.7 copy-start.1
  4.1 0.7 copy-start.2
  4.8 0.7 copy-start.3
  5.5 0.7 copy-start.4

commit v2 on v1

--- a/solution.py
+++ b/solution.py
@@ -17,6 +17,14 @@
 HALF = 128
 ROWS = SLABS * CHIPS
 BLOCK = 8
+TURNS = sorted(
+    ((dx, dy) for dx in range(SIDE) for dy in range(SIDE)),
+    key=lambda turn: -sum(min(step, SIDE - step) for step in turn),
+)
+CHIP_STEPS = TURNS[:-1]
+PLANE_STEPS = [(dx, dy, dc) for dx, dy in TURNS for dc in (1, 0)][:-1]
+SLAB_STEPS = [4, 3, 5, 2, 6, 1, 7]
+PLACE_STEPS = [(dz, dc) for dz in SLAB_STEPS for dc in range(CORES)] + [(0, 1)]
 F32 = jnp.float32
 BF16 = jnp.bfloat16
 
@@ -91,10 +99,10 @@
 
 
 def kernel(
-    tensor, signs3, picked3, signs2, picked2, out,
-    slabs, table3, table2, outgoing, landed, sketch, spread, slices, planes,
+    tensor, signs3_in, picked3_in, signs2_in, picked2_in, out,
+    signs3, picked3, signs2, picked2, slabs, table3, table2, outgoing, landed, sketch, spread, slices, planes,
     partial_gram, terms, row_block, blocks, block, gram, result, returned,
-    load_sem, send_sem, recv_sem, spread_send, spread_recv, slice_send, slice_recv,
+    small_sem, load_sem, send_sem, recv_sem, spread_send, spread_recv, slice_send, slice_recv,
     term_send, term_recv, block_send, block_recv, gram_send, gram_recv, back_send, back_recv,
 ):
     z = lax.axis_index("slab")
@@ -103,30 +111,40 @@
     h = p % CORES
     x, y = q // SIDE, q % SIDE
 
-    def shifted(step, sign):
-        turn = (step + 1) % CHIPS
-        dx, dy = turn // SIDE, turn % SIDE
-        return ((x + sign * dx + SIDE) % SIDE) * SIDE + (y + sign * dy + SIDE) % SIDE
+    def chip_at(dx, dy):
+        return ((x + dx) & (SIDE - 1)) * SIDE + ((y + dy) & (SIDE - 1))
+
+    def device_at(dx, dy, dc):
+        return chip_at(dx, dy) * CORES + (h ^ dc)
+
+    def slab_at(dz):
+        return (z + dz) & (SLABS - 1)
+
+    barrier = pltpu.get_barrier_semaphore()
+    for step in PLANE_STEPS:
+        pl.semaphore_signal(barrier, 1, device_id=(z, device_at(*step)), device_id_type=MESH)
+    for dz, dc in PLACE_STEPS[:-1]:
+        pl.semaphore_signal(
+            barrier, 1, device_id=(slab_at(dz), q * CORES + (h ^ dc)), device_id_type=MESH
+        )
 
     def load(step):
-        return pltpu.make_async_copy(tensor.at[shifted(step, 1)], slabs.at[step], load_sem.at[step])
-
-    @pl.loop(0, CHIPS)
-    def _(step):
+        return pltpu.make_async_copy(tensor.at[chip_at(*TURNS[step])], slabs.at[step], load_sem.at[step])
+
+    small = [
+        pltpu.make_async_copy(source, target, small_sem.at[n])
+        for n, (source, target) in enumerate(
+            [(picked3_in, picked3), (picked2_in, picked2), (signs2_in, signs2), (signs3_in, signs3)]
+        )
+    ]
+    for copy in small:
+        copy.start()
+
+    for step in range(CHIPS):
         load(step).start()
 
-    barrier = pltpu.get_barrier_semaphore()
-
-    @pl.loop(1, COLS)
-    def _(step):
-        pl.semaphore_signal(barrier, 1, device_id=(z, (p + step) % COLS), device_id_type=MESH)
-
-    @pl.loop(1, SLABS)
-    def _(step):
-        for core in range(CORES):
-            pl.semaphore_signal(
-                barrier, 1, device_id=((z + step) % SLABS, q * CORES + core), device_id_type=MESH
-            )
+    for copy in small:
+        copy.wait()
 
     below = lax.broadcasted_iota(jnp.int32, (HALF, HALF), 0)
     for half in range(RANK // HALF):
@@ -147,24 +165,20 @@
             signs = signs2[tile : tile + 1, :].astype(F32)
             table2[tile, half * HALF : (half + 1) * HALF, :] = (low * high * signs).astype(BF16)
 
-    pl.semaphore_wait(barrier, COLS - 1 + (SLABS - 1) * CORES)
-
     def piece(step, core):
-        chip = shifted(step, 1)
         return pltpu.make_async_remote_copy(
             outgoing.at[step, core],
             landed.at[p],
             send_sem.at[step, core],
             recv_sem.at[p],
-            device_id=(z, chip * CORES + core),
-            device_id_type=MESH,
-        )
-
-    @pl.loop(0, CHIPS, step=2)
-    def _(step):
+            device_id=(z, chip_at(*TURNS[step]) * CORES + core),
+            device_id_type=MESH,
+        )
+
+    for step in range(0, CHIPS, 2):
         load(step).wait()
         load(step + 1).wait()
-        both = slabs[pl.ds(step, 2)].reshape(2 * WIDTH, LENGTH)
+        both = slabs[step : step + 2].reshape(2 * WIDTH, LENGTH)
         highs, lows = [], []
         for tile in range(LENGTH // HALF):
             signs = signs3[tile : tile + 1, :].astype(F32)
@@ -181,17 +195,14 @@
                 outgoing[step + part, core] = first[
                     part * WIDTH : (part + 1) * WIDTH, core * HALF : (core + 1) * HALF
                 ]
-        for core in range(CORES):
-            piece(step, core).start()
-
-        @pl.when(step + 1 < CHIPS - 1)
-        def _():
-            for core in range(CORES):
-                piece(step + 1, core).start()
-
-        @pl.when(step + 1 == CHIPS - 1)
-        def _():
-            piece(step + 1, 1 - h).start()
+        if step == 0:
+            pl.semaphore_wait(barrier, len(PLANE_STEPS) + len(PLACE_STEPS) - 1)
+        for part in range(2):
+            if step + part < CHIPS - 1:
+                for core in range(CORES):
+                    piece(step + part, core).start()
+            else:
+                piece(step + part, 1 - h).start()
 
     landed[p] = outgoing[CHIPS - 1, h]
 
@@ -205,36 +216,28 @@
             device_id_type=MESH,
         )
 
-    def two_chips(step, total):
+    total = jnp.zeros((RANK, 2 * HALF), F32)
+    for step in range(0, CHIPS, 2):
         lefts, rights = [], []
-        for part in range(2):
-            chip = shifted(step + part, -1)
-
-            @pl.when(step + part < CHIPS - 1)
-            def _():
+        for dx, dy in TURNS[step : step + 2]:
+            chip = chip_at(-dx, -dy)
+            if dx or dy:
                 for core in range(CORES):
                     arrival(chip * CORES + core).wait_recv()
-
-            @pl.when(step + part == CHIPS - 1)
-            def _():
+            else:
                 arrival(p ^ 1).wait_recv()
-
             lefts.append(table2[chip])
             value = landed[pl.ds(chip * CORES, CORES)].reshape(CORES * WIDTH, HALF)
             rights.append(jnp.concatenate(split_two(value), axis=1))
-        return total + jnp.dot(
+        total = total + jnp.dot(
             jnp.concatenate(lefts, axis=1),
             jnp.concatenate(rights, axis=0),
             preferred_element_type=F32,
         )
-
-    total = lax.fori_loop(
-        0, CHIPS // 2, lambda n, t: two_chips(2 * n, t), jnp.zeros((RANK, 2 * HALF), F32)
-    )
     sketch[...] = (total[:, :HALF] + total[:, HALF:]).reshape(COLS, RANK // COLS, HALF)
 
     def row_copy(step):
-        to = (p + step) % COLS
+        to = device_at(*PLANE_STEPS[step])
         return pltpu.make_async_remote_copy(
             sketch.at[to],
             spread.at[q, h],
@@ -245,7 +248,7 @@
         )
 
     def row_arrival(step):
-        source = (p + step) % COLS
+        source = device_at(*PLANE_STEPS[step])
         return pltpu.make_async_remote_copy(
             sketch.at[source],
             spread.at[source // CORES, source % CORES],
@@ -255,14 +258,12 @@
             device_id_type=MESH,
         )
 
-    @pl.loop(1, COLS)
-    def _(step):
+    for step in range(len(PLANE_STEPS)):
         row_copy(step).start()
 
     spread[q, h] = sketch[p]
 
-    @pl.loop(1, COLS)
-    def _(step):
+    for step in range(len(PLANE_STEPS)):
         row_arrival(step).wait_recv()
 
     for core in range(CORES):
@@ -270,7 +271,7 @@
             slices[r, :, core * HALF : (core + 1) * HALF] = spread[:, core, r, :]
 
     def slice_copy(step):
-        to = (z + step) % SLABS
+        to = slab_at(SLAB_STEPS[step])
         return pltpu.make_async_remote_copy(
             slices.at[to],
             planes.at[z],
@@ -281,7 +282,7 @@
         )
 
     def slice_arrival(step):
-        source = (z + step) % SLABS
+        source = slab_at(SLAB_STEPS[step])
         return pltpu.make_async_remote_copy(
             slices.at[source],
             planes.at[source],
@@ -291,21 +292,19 @@
             device_id_type=MESH,
         )
 
-    @pl.loop(1, SLABS)
-    def _(step):
+    for step in range(len(SLAB_STEPS)):
         slice_copy(step).start()
 
     planes[z] = slices[z]
 
-    @pl.loop(1, SLABS)
-    def _(step):
+    for step in range(len(SLAB_STEPS)):
         slice_arrival(step).wait_recv()
 
     flat = planes[...].reshape(ROWS, RANK)
     partial_gram[...] = exact_dot(flat, flat, ((1,), (1,))).reshape(CHIPS, BLOCK, ROWS)
 
     def term_copy(step):
-        to = (q + step) % CHIPS
+        to = chip_at(*CHIP_STEPS[step])
         return pltpu.make_async_remote_copy(
             partial_gram.at[to],
             terms.at[q],
@@ -316,7 +315,7 @@
         )
 
     def term_arrival(step):
-        source = (q + step) % CHIPS
+        source = chip_at(*CHIP_STEPS[step])
         return pltpu.make_async_remote_copy(
             partial_gram.at[source],
             terms.at[source],
@@ -326,57 +325,53 @@
             device_id_type=MESH,
         )
 
-    @pl.loop(1, CHIPS)
-    def _(step):
+    for step in range(len(CHIP_STEPS)):
         term_copy(step).start()
 
     terms[q] = partial_gram[q]
 
-    @pl.loop(1, CHIPS)
-    def _(step):
+    for step in range(len(CHIP_STEPS)):
         term_arrival(step).wait_recv()
 
     row_block[...] = jnp.sum(terms[...], axis=0)
 
     place = z * CORES + h
-    places = SLABS * CORES
 
     def block_copy(step):
-        to = (place + step) % places
+        dz, dc = PLACE_STEPS[step]
         return pltpu.make_async_remote_copy(
             row_block,
             blocks.at[place],
             block_send.at[step],
             block_recv.at[place],
-            device_id=(to // CORES, q * CORES + to % CORES),
+            device_id=(slab_at(dz), q * CORES + (h ^ dc)),
             device_id_type=MESH,
         )
 
     def block_arrival(step):
-        source = (place + step) % places
+        dz, dc = PLACE_STEPS[step]
+        source = slab_at(dz) * CORES + (h ^ dc)
         return pltpu.make_async_remote_copy(
             row_block,
             blocks.at[source],
             block_send.at[step],
             block_recv.at[source],
-            device_id=(source // CORES, q * CORES + source % CORES),
-            device_id_type=MESH,
-        )
-
-    @pl.loop(1, places)
-    def _(step):
+            device_id=(slab_at(dz), q * CORES + (h ^ dc)),
+            device_id_type=MESH,
+        )
+
+    for step in range(len(PLACE_STEPS)):
         block_copy(step).start()
 
     blocks[place] = row_block[...]
 
-    @pl.loop(1, places)
-    def _(step):
+    for step in range(len(PLACE_STEPS)):
         block_arrival(step).wait_recv()
 
     block[...] = jnp.sum(blocks[...], axis=0)
 
     def gram_copy(step):
-        to = (q + step) % CHIPS
+        to = chip_at(*CHIP_STEPS[step])
         return pltpu.make_async_remote_copy(
             block,
             gram.at[pl.ds(q * BLOCK, BLOCK)],
@@ -387,7 +382,7 @@
         )
 
     def gram_arrival(step):
-        source = (q + step) % CHIPS
+        source = chip_at(*CHIP_STEPS[step])
         return pltpu.make_async_remote_copy(
             block,
             gram.at[pl.ds(source * BLOCK, BLOCK)],
@@ -397,14 +392,12 @@
             device_id_type=MESH,
         )
 
-    @pl.loop(1, CHIPS)
-    def _(step):
+    for step in range(len(CHIP_STEPS)):
         gram_copy(step).start()
 
     gram[pl.ds(pl.multiple_of(q * BLOCK, BLOCK), BLOCK), :] = block[...]
 
-    @pl.loop(1, CHIPS)
-    def _(step):
+    for step in range(len(CHIP_STEPS)):
         gram_arrival(step).wait_recv()
 
     inverse_factor(gram)
@@ -415,7 +408,7 @@
     result[...] = exact_dot(inverse, flat, ((1,), (0,))).reshape(SLABS, CHIPS, RANK)
 
     def back_copy(step):
-        to = (z + step) % SLABS
+        to = slab_at(SLAB_STEPS[step])
         return pltpu.make_async_remote_copy(
             result.at[to],
             returned.at[z],
@@ -426,7 +419,7 @@
         )
 
     def back_arrival(step):
-        source = (z + step) % SLABS
+        source = slab_at(SLAB_STEPS[step])
         return pltpu.make_async_remote_copy(
             result.at[source],
             returned.at[source],
@@ -436,36 +429,30 @@
             device_id_type=MESH,
         )
 
-    @pl.loop(1, SLABS)
-    def _(step):
+    for step in range(len(SLAB_STEPS)):
         back_copy(step).start()
 
     out[z] = result[z]
 
-    @pl.loop(1, SLABS)
-    def _(step):
+    for step in range(len(SLAB_STEPS)):
         back_arrival(step).wait_recv()
-        source = (z + step) % SLABS
+        source = slab_at(SLAB_STEPS[step])
         out[source] = returned[source]
 
-    @pl.loop(0, CHIPS - 1)
-    def _(step):
+    for step in range(CHIPS - 1):
         for core in range(CORES):
             piece(step, core).wait_send()
 
     piece(CHIPS - 1, 1 - h).wait_send()
 
-    @pl.loop(1, COLS)
-    def _(step):
+    for step in range(len(PLANE_STEPS)):
         row_copy(step).wait_send()
 
-    @pl.loop(1, SLABS)
-    def _(step):
+    for step in range(len(SLAB_STEPS)):
         slice_copy(step).wait_send()
         back_copy(step).wait_send()
 
-    @pl.loop(1, CHIPS)
-    def _(step):
+    for step in range(len(CHIP_STEPS)):
         term_copy(step).wait_send()
         block_copy(step).wait_send()
         gram_copy(step).wait_send()
@@ -478,9 +465,13 @@
     return pl.pallas_call(
         kernel,
         out_shape=jax.ShapeDtypeStruct((RANK // COLS, CHIPS, RANK), F32),
-        in_specs=[pl.BlockSpec(memory_space=pl.ANY)] + [vmem] * 4,
+        in_specs=[pl.BlockSpec(memory_space=pl.ANY)] * 5,
         out_specs=vmem,
         scratch_shapes=[
+            pltpu.VMEM((LENGTH // HALF, HALF), jnp.int32),
+            pltpu.VMEM((RANK // HALF, HALF), jnp.int32),
+            pltpu.VMEM((CHIPS, HALF), jnp.int32),
+            pltpu.VMEM((RANK // HALF, HALF), jnp.int32),
             pltpu.VMEM((CHIPS, WIDTH, LENGTH), F32),
             pltpu.VMEM((LENGTH, RANK), BF16),
             pltpu.VMEM((CHIPS, RANK, HALF), BF16),
@@ -498,6 +489,7 @@
             pltpu.VMEM((ROWS, ROWS), F32),
             pltpu.VMEM((SLABS, CHIPS, RANK), F32),
             pltpu.VMEM((SLABS, CHIPS, RANK), F32),
+            dma((4,)),
             dma((CHIPS,)),
             dma((CHIPS, CORES)),
             dma((COLS,)),
@@ -515,7 +507,7 @@
             dma((SLABS,)),
         ],
         compiler_params=pltpu.CompilerParams(
-            collective_id=0, has_side_effects=True, vmem_limit_bytes=40 * 1024 * 1024
+            collective_id=0, has_side_effects=True, vmem_limit_bytes=64 * 1024 * 1024
         ),
         name="sketch_basis",
     )(

time: 77.5 us -> 65.7 us (0.85)
  Pallas kernels: 70.3 us -> 64 us
  local copies, waits for them, and re-layouts: 6.79 us -> 1.57 us
    pallas_call x1, Pallas kernels: 70.3 us -> 64 us  [on_device(): pl.pallas_call(kernel, out_shape=jax.ShapeDtypeStruct((RANK // COLS, CHIP...]
    unnamed x11 -> x1, local copies, waits for them, and re-layouts: 6.79 us -> 1.57 us
where the time goes in v2:
time: 65.7 us; the launch traced here: 65.6 us
  Pallas kernels  64 us (97%)
  local copies, waits for them, and re-layouts  1.57 us (2%)
    pallas_call x1, Pallas kernels, on_device(): pl.pallas_call(kernel, out_shape=jax.ShapeDtypeStruct((RANK // COLS, CHIP...  64 us
    unnamed x1, local copies, waits for them, and re-layouts  1.57 us

profile of v2, /device:TPU:1, one launch (start us, length us, event | category | flops | bytes accessed | tf_op | source)
XLA Modules:
  0.0 65.6 jit_solution(6319366018128269228)
XLA Ops:
  0.0 64.0 %sketch_basis.1 = f32[8,16,256]{2,1,0:T(8,128)} custom-call(f32[16,64,2048]{2,1,0:T(8,128)} %tensor.1, s32[16,128]{1,0:T(8,128)} %bitcast.4, s32[2,128]{1,0:T(2,128)} %bitcast.6, s32[16,128]{1,0:T(8,128)} %bitcast.5, s32[2,128]{1,0:T(2,128)} %bitcast.7), custom_call_target="tpu_custom_call" | custom-call | tf_op jit(solution)/shard_map/sketch_basis/pallas_call | solution.py:465
  64.0 1.6 %copy.7 = f32[8,16,256]{2,1,0:T(8,128)} copy(f32[8,16,256]{2,1,0:T(8,128)} %sketch_basis.1) | data formatting | bytes 262144

commit v3 on v2

--- a/solution.py
+++ b/solution.py
@@ -25,6 +25,10 @@
 PLANE_STEPS = [(dx, dy, dc) for dx, dy in TURNS for dc in (1, 0)][:-1]
 SLAB_STEPS = [4, 3, 5, 2, 6, 1, 7]
 PLACE_STEPS = [(dz, dc) for dz in SLAB_STEPS for dc in range(CORES)] + [(0, 1)]
+PAIRS = CHIPS // 2
+CHUNKS = 2
+GROUP = PAIRS // CHUNKS
+LOADS = [n + PAIRS * part for n in range(PAIRS) for part in range(2)]
 F32 = jnp.float32
 BF16 = jnp.bfloat16
 
@@ -100,9 +104,9 @@
 
 def kernel(
     tensor, signs3_in, picked3_in, signs2_in, picked2_in, out,
-    signs3, picked3, signs2, picked2, slabs, table3, table2, outgoing, landed, sketch, spread, slices, planes,
-    partial_gram, terms, row_block, blocks, block, gram, result, returned,
-    small_sem, load_sem, send_sem, recv_sem, spread_send, spread_recv, slice_send, slice_recv,
+    signs3, picked3, signs2, picked2, slabs, table3, table2, outgoing, landed, sketch, slices, planes,
+    columns, spread, row_slices, row_planes, partial_gram, terms, row_block, blocks, block, gram, result,
+    small_sem, load_sem, send_sem, recv_sem, slice_send, slice_recv, spread_send, spread_recv, row_send, row_recv,
     term_send, term_recv, block_send, block_recv, gram_send, gram_recv, back_send, back_recv,
 ):
     z = lax.axis_index("slab")
@@ -129,7 +133,7 @@
         )
 
     def load(step):
-        return pltpu.make_async_copy(tensor.at[chip_at(*TURNS[step])], slabs.at[step], load_sem.at[step])
+        return pltpu.make_async_copy(tensor.at[step], slabs.at[step], load_sem.at[step])
 
     small = [
         pltpu.make_async_copy(source, target, small_sem.at[n])
@@ -140,7 +144,7 @@
     for copy in small:
         copy.start()
 
-    for step in range(CHIPS):
+    for step in LOADS:
         load(step).start()
 
     for copy in small:
@@ -155,30 +159,32 @@
             table3[tile * HALF : (tile + 1) * HALF, half * HALF : (half + 1) * HALF] = (
                 low * high
             ).astype(BF16)
-    along = lax.broadcasted_iota(jnp.int32, (HALF, HALF), 1)
     for half in range(RANK // HALF):
-        picks = picked2[half : half + 1, :].astype(F32)
-        picks = jnp.broadcast_to(picks, (HALF, HALF)).T.astype(jnp.int32)
-        low = odd(along & picks)
+        picks = picked2[half : half + 1, :]
+        low = odd(below & jnp.broadcast_to(picks, (HALF, HALF)))
         for tile in range(CHIPS):
-            high = odd(picks & (tile * HALF))
-            signs = signs2[tile : tile + 1, :].astype(F32)
-            table2[tile, half * HALF : (half + 1) * HALF, :] = (low * high * signs).astype(BF16)
-
-    def piece(step, core):
-        return pltpu.make_async_remote_copy(
-            outgoing.at[step, core],
-            landed.at[p],
-            send_sem.at[step, core],
-            recv_sem.at[p],
-            device_id=(z, chip_at(*TURNS[step]) * CORES + core),
-            device_id_type=MESH,
-        )
-
-    for step in range(0, CHIPS, 2):
-        load(step).wait()
-        load(step + 1).wait()
-        both = slabs[step : step + 2].reshape(2 * WIDTH, LENGTH)
+            high = odd(jnp.broadcast_to(picks, (BLOCK, HALF)) & (tile * HALF))[:1]
+            table2[tile, :, half * HALF : (half + 1) * HALF] = (low * high).astype(BF16)
+
+    def piece(chunk, step):
+        to = device_at(*PLANE_STEPS[step])
+        part = pl.ds(chunk * GROUP, GROUP)
+        return pltpu.make_async_remote_copy(
+            outgoing.at[to, part],
+            landed.at[p, part],
+            send_sem.at[chunk, step],
+            recv_sem.at[chunk, p],
+            device_id=(z, to),
+            device_id_type=MESH,
+        )
+
+    for chunk in range(CHUNKS):
+        start = chunk * GROUP
+        for step in LOADS[2 * start : 2 * (start + GROUP)]:
+            load(step).wait()
+        both = jnp.concatenate(
+            [slabs[start : start + GROUP], slabs[PAIRS + start : PAIRS + start + GROUP]], axis=0
+        ).reshape(GROUP * HALF, LENGTH)
         highs, lows = [], []
         for tile in range(LENGTH // HALF):
             signs = signs3[tile : tile + 1, :].astype(F32)
@@ -189,86 +195,65 @@
             [jnp.concatenate(highs, axis=1), jnp.concatenate(lows, axis=1)], axis=0
         )
         first = jnp.dot(left, table3[...], preferred_element_type=F32)
-        first = first[: 2 * WIDTH] + first[2 * WIDTH :]
-        for part in range(2):
-            for core in range(CORES):
-                outgoing[step + part, core] = first[
-                    part * WIDTH : (part + 1) * WIDTH, core * HALF : (core + 1) * HALF
-                ]
-        if step == 0:
+        first = first[: GROUP * HALF] + first[GROUP * HALF :]
+        first = first.reshape(2, GROUP, WIDTH, RANK)
+        for pair in range(GROUP):
+            for half in range(CORES):
+                turned = first[:, pair, :, half * HALF : (half + 1) * HALF].reshape(HALF, HALF).T
+                outgoing[half * CHIPS : (half + 1) * CHIPS, start + pair] = turned.reshape(
+                    CHIPS, BLOCK, HALF
+                )
+        if chunk == 0:
             pl.semaphore_wait(barrier, len(PLANE_STEPS) + len(PLACE_STEPS) - 1)
-        for part in range(2):
-            if step + part < CHIPS - 1:
-                for core in range(CORES):
-                    piece(step + part, core).start()
-            else:
-                piece(step + part, 1 - h).start()
-
-    landed[p] = outgoing[CHIPS - 1, h]
+        for step in range(len(PLANE_STEPS)):
+            piece(chunk, step).start()
+
+    landed[p] = outgoing[p]
 
     def arrival(source):
-        return pltpu.make_async_remote_copy(
-            outgoing.at[0, 0],
-            landed.at[source],
-            send_sem.at[0, 0],
-            recv_sem.at[source],
-            device_id=(z, p ^ 1),
-            device_id_type=MESH,
-        )
-
-    total = jnp.zeros((RANK, 2 * HALF), F32)
+        for chunk in range(CHUNKS):
+            part = pl.ds(chunk * GROUP, GROUP)
+            pltpu.make_async_remote_copy(
+                outgoing.at[source, part],
+                landed.at[source, part],
+                send_sem.at[chunk, 0],
+                recv_sem.at[chunk, source],
+                device_id=(z, p ^ 1),
+                device_id_type=MESH,
+            ).wait_recv()
+
+    lane = lax.broadcasted_iota(jnp.int32, (WIDTH, HALF), 1)
+    total = jnp.zeros((2 * HALF, RANK), F32)
     for step in range(0, CHIPS, 2):
         lefts, rights = [], []
         for dx, dy in TURNS[step : step + 2]:
             chip = chip_at(-dx, -dy)
             if dx or dy:
                 for core in range(CORES):
-                    arrival(chip * CORES + core).wait_recv()
+                    arrival(chip * CORES + core)
             else:
-                arrival(p ^ 1).wait_recv()
-            lefts.append(table2[chip])
-            value = landed[pl.ds(chip * CORES, CORES)].reshape(CORES * WIDTH, HALF)
-            rights.append(jnp.concatenate(split_two(value), axis=1))
+                arrival(p ^ 1)
+            even = landed[chip * CORES].reshape(WIDTH, HALF)
+            odds = landed[chip * CORES + 1].reshape(WIDTH, HALF)
+            value = jnp.concatenate(
+                [
+                    jnp.where(lane < WIDTH, even, pltpu.roll(odds, WIDTH, 1)),
+                    jnp.where(lane < WIDTH, pltpu.roll(even, WIDTH, 1), odds),
+                ],
+                axis=0,
+            )
+            value = value * signs2[pl.ds(chip, 1), :].astype(F32)
+            lefts.append(jnp.concatenate(split_two(value), axis=0))
+            rights.append(table2[chip])
         total = total + jnp.dot(
             jnp.concatenate(lefts, axis=1),
             jnp.concatenate(rights, axis=0),
             preferred_element_type=F32,
         )
-    sketch[...] = (total[:, :HALF] + total[:, HALF:]).reshape(COLS, RANK // COLS, HALF)
-
-    def row_copy(step):
-        to = device_at(*PLANE_STEPS[step])
-        return pltpu.make_async_remote_copy(
-            sketch.at[to],
-            spread.at[q, h],
-            spread_send.at[step],
-            spread_recv.at[p],
-            device_id=(z, to),
-            device_id_type=MESH,
-        )
-
-    def row_arrival(step):
-        source = device_at(*PLANE_STEPS[step])
-        return pltpu.make_async_remote_copy(
-            sketch.at[source],
-            spread.at[source // CORES, source % CORES],
-            spread_send.at[step],
-            spread_recv.at[source],
-            device_id=(z, source),
-            device_id_type=MESH,
-        )
-
-    for step in range(len(PLANE_STEPS)):
-        row_copy(step).start()
-
-    spread[q, h] = sketch[p]
-
-    for step in range(len(PLANE_STEPS)):
-        row_arrival(step).wait_recv()
-
-    for core in range(CORES):
-        for r in range(SLABS):
-            slices[r, :, core * HALF : (core + 1) * HALF] = spread[:, core, r, :]
+    sketch[...] = (total[:HALF] + total[HALF:]).reshape(2, PAIRS, BLOCK, RANK)
+    for column in range(BLOCK):
+        for part in range(2):
+            slices[column, part * PAIRS : (part + 1) * PAIRS, :] = sketch[part, :, column, :]
 
     def slice_copy(step):
         to = slab_at(SLAB_STEPS[step])
@@ -330,6 +315,38 @@
 
     terms[q] = partial_gram[q]
 
+    across = slices[...].reshape(HALF, RANK)
+    for half in range(CORES):
+        turned = across[:, half * HALF : (half + 1) * HALF].T
+        columns[half * CHIPS : (half + 1) * CHIPS] = turned.reshape(CHIPS, BLOCK, HALF)
+
+    def row_copy(step):
+        to = device_at(*PLANE_STEPS[step])
+        return pltpu.make_async_remote_copy(
+            columns.at[to],
+            spread.at[p],
+            spread_send.at[step],
+            spread_recv.at[p],
+            device_id=(z, to),
+            device_id_type=MESH,
+        )
+
+    def row_arrival(step):
+        source = device_at(*PLANE_STEPS[step])
+        return pltpu.make_async_remote_copy(
+            columns.at[source],
+            spread.at[source],
+            spread_send.at[step],
+            spread_recv.at[source],
+            device_id=(z, source),
+            device_id_type=MESH,
+        )
+
+    for step in range(len(PLANE_STEPS)):
+        row_copy(step).start()
+
+    spread[p] = columns[p]
+
     for step in range(len(CHIP_STEPS)):
         term_arrival(step).wait_recv()
 
@@ -365,6 +382,50 @@
 
     blocks[place] = row_block[...]
 
+    for step in range(len(PLANE_STEPS)):
+        row_arrival(step).wait_recv()
+    source_row = lax.broadcasted_iota(jnp.int32, (COLS, RANK), 0)
+    source_lane = lax.broadcasted_iota(jnp.int32, (COLS, RANK), 1)
+    repeat = jnp.where(source_lane // BLOCK == source_row, F32(1), F32(0)).astype(BF16)
+    repeat = jnp.concatenate([repeat] * 3, axis=0)
+    kind = lax.broadcasted_iota(jnp.int32, (CHIPS, RANK), 1) % BLOCK
+    for r in range(BLOCK):
+        thirds = jnp.concatenate(split_three(spread[:, r, :]), axis=0)
+        wide = lax.dot_general(
+            thirds, repeat, (((0,), (0,)), ((), ())), preferred_element_type=F32
+        ).reshape(BLOCK, CHIPS, RANK)
+        chosen = wide[0]
+        for column in range(1, BLOCK):
+            chosen = jnp.where(kind == column, wide[column], chosen)
+        row_slices[r] = chosen
+
+    def row_slice_copy(step):
+        to = slab_at(SLAB_STEPS[step])
+        return pltpu.make_async_remote_copy(
+            row_slices.at[to],
+            row_planes.at[z],
+            row_send.at[step],
+            row_recv.at[z],
+            device_id=(to, p),
+            device_id_type=MESH,
+        )
+
+    def row_slice_arrival(step):
+        source = slab_at(SLAB_STEPS[step])
+        return pltpu.make_async_remote_copy(
+            row_slices.at[source],
+            row_planes.at[source],
+            row_send.at[step],
+            row_recv.at[source],
+            device_id=(source, p),
+            device_id_type=MESH,
+        )
+
+    for step in range(len(SLAB_STEPS)):
+        row_slice_copy(step).start()
+
+    row_planes[z] = row_slices[z]
+
     for step in range(len(PLACE_STEPS)):
         block_arrival(step).wait_recv()
 
@@ -405,13 +466,16 @@
     row = lax.broadcasted_iota(jnp.int32, (ROWS, ROWS), 0)
     col = lax.broadcasted_iota(jnp.int32, (ROWS, ROWS), 1)
     inverse = jnp.where(col <= row, gram[...], F32(0)) * F32(RANK)
-    result[...] = exact_dot(inverse, flat, ((1,), (0,))).reshape(SLABS, CHIPS, RANK)
+    for step in range(len(SLAB_STEPS)):
+        row_slice_arrival(step).wait_recv()
+    rows = row_planes[...].reshape(ROWS, RANK)
+    result[...] = exact_dot(inverse, rows, ((1,), (0,))).reshape(SLABS, CHIPS, RANK)
 
     def back_copy(step):
         to = slab_at(SLAB_STEPS[step])
         return pltpu.make_async_remote_copy(
             result.at[to],
-            returned.at[z],
+            out.at[z],
             back_send.at[step],
             back_recv.at[z],
             device_id=(to, p),
@@ -422,7 +486,7 @@
         source = slab_at(SLAB_STEPS[step])
         return pltpu.make_async_remote_copy(
             result.at[source],
-            returned.at[source],
+            out.at[source],
             back_send.at[step],
             back_recv.at[source],
             device_id=(source, p),
@@ -432,24 +496,22 @@
     for step in range(len(SLAB_STEPS)):
         back_copy(step).start()
 
-    out[z] = result[z]
-
+    own = pltpu.make_async_copy(result.at[z], out.at[z], back_send.at[len(SLAB_STEPS)])
+    own.start()
     for step in range(len(SLAB_STEPS)):
         back_arrival(step).wait_recv()
-        source = slab_at(SLAB_STEPS[step])
-        out[source] = returned[source]
-
-    for step in range(CHIPS - 1):
-        for core in range(CORES):
-            piece(step, core).wait_send()
-
-    piece(CHIPS - 1, 1 - h).wait_send()
+    own.wait()
+
+    for step in range(len(PLANE_STEPS)):
+        for chunk in range(CHUNKS):
+            piece(chunk, step).wait_send()
 
     for step in range(len(PLANE_STEPS)):
         row_copy(step).wait_send()
 
     for step in range(len(SLAB_STEPS)):
         slice_copy(step).wait_send()
+        row_slice_copy(step).wait_send()
         back_copy(step).wait_send()
 
     for step in range(len(CHIP_STEPS)):
@@ -459,14 +521,13 @@
 
 
 def on_device(tensor, signs3, picked3, signs2, picked2):
-    vmem = pl.BlockSpec(memory_space=pltpu.VMEM)
     dma = pltpu.SemaphoreType.DMA
     places = SLABS * CORES
     return pl.pallas_call(
         kernel,
         out_shape=jax.ShapeDtypeStruct((RANK // COLS, CHIPS, RANK), F32),
         in_specs=[pl.BlockSpec(memory_space=pl.ANY)] * 5,
-        out_specs=vmem,
+        out_specs=pl.BlockSpec(memory_space=pl.ANY),
         scratch_shapes=[
             pltpu.VMEM((LENGTH // HALF, HALF), jnp.int32),
             pltpu.VMEM((RANK // HALF, HALF), jnp.int32),
@@ -474,11 +535,14 @@
             pltpu.VMEM((RANK // HALF, HALF), jnp.int32),
             pltpu.VMEM((CHIPS, WIDTH, LENGTH), F32),
             pltpu.VMEM((LENGTH, RANK), BF16),
-            pltpu.VMEM((CHIPS, RANK, HALF), BF16),
-            pltpu.VMEM((CHIPS, CORES, WIDTH, HALF), F32),
-            pltpu.VMEM((COLS, WIDTH, HALF), F32),
-            pltpu.VMEM((COLS, RANK // COLS, HALF), F32),
-            pltpu.VMEM((CHIPS, CORES, RANK // COLS, HALF), F32),
+            pltpu.VMEM((CHIPS, HALF, RANK), BF16),
+            pltpu.VMEM((COLS, PAIRS, BLOCK, HALF), F32),
+            pltpu.VMEM((COLS, PAIRS, BLOCK, HALF), F32),
+            pltpu.VMEM((2, PAIRS, BLOCK, RANK), F32),
+            pltpu.VMEM((SLABS, CHIPS, RANK), F32),
+            pltpu.VMEM((SLABS, CHIPS, RANK), F32),
+            pltpu.VMEM((COLS, BLOCK, HALF), F32),
+            pltpu.VMEM((COLS, BLOCK, HALF), F32),
             pltpu.VMEM((SLABS, CHIPS, RANK), F32),
             pltpu.VMEM((SLABS, CHIPS, RANK), F32),
             pltpu.VMEM((CHIPS, BLOCK, ROWS), F32),
@@ -488,11 +552,12 @@
             pltpu.VMEM((BLOCK, ROWS), F32),
             pltpu.VMEM((ROWS, ROWS), F32),
             pltpu.VMEM((SLABS, CHIPS, RANK), F32),
-            pltpu.VMEM((SLABS, CHIPS, RANK), F32),
             dma((4,)),
             dma((CHIPS,)),
-            dma((CHIPS, CORES)),
-            dma((COLS,)),
+            dma((CHUNKS, COLS)),
+            dma((CHUNKS, COLS)),
+            dma((SLABS,)),
+            dma((SLABS,)),
             dma((COLS,)),
             dma((COLS,)),
             dma((SLABS,)),

time: 65.7 us -> 62.9 us (0.957)
  Pallas kernels: 64 us -> 61 us
    pallas_call x1, Pallas kernels: 64 us -> 61 us  [on_device(): pl.pallas_call(kernel, out_shape=jax.ShapeDtypeStruct((RANK // COLS, CHIP...]
where the time goes in v3:
time: 62.9 us; the launch traced here: 62.6 us
  Pallas kernels  61 us (97%)
  local copies, waits for them, and re-layouts  1.57 us (2%)
    pallas_call x1, Pallas kernels, on_device(): pl.pallas_call(kernel, out_shape=jax.ShapeDtypeStruct((RANK // COLS, CHIP...  61 us
    unnamed x1, local copies, waits for them, and re-layouts  1.57 us

profile of v3, /device:TPU:1, one launch (start us, length us, event | category | flops | bytes accessed | tf_op | source)
XLA Modules:
  0.0 62.6 jit_solution(7683071172834813897)
XLA Ops:
  0.0 61.0 %sketch_basis.1 = f32[8,16,256]{2,1,0:T(8,128)} custom-call(f32[16,64,2048]{2,1,0:T(8,128)} %tensor.1, s32[16,128]{1,0:T(8,128)} %bitcast.4, s32[2,128]{1,0:T(2,128)} %bitcast.6, s32[16,128]{1,0:T(8,128)} %bitcast.5, s32[2,128]{1,0:T(2,128)} %bitcast.7), custom_call_target="tpu_custom_call" | custom-call | tf_op jit(solution)/shard_map/sketch_basis/pallas_call | solution.py:526
  61.1 1.6 %copy.7 = f32[8,16,256]{2,1,0:T(8,128)} copy(f32[8,16,256]{2,1,0:T(8,128)} %sketch_basis.1) | data formatting | bytes 262144

commit v4 on v3

--- a/solution.py
+++ b/solution.py
@@ -26,8 +26,9 @@
 SLAB_STEPS = [4, 3, 5, 2, 6, 1, 7]
 PLACE_STEPS = [(dz, dc) for dz in SLAB_STEPS for dc in range(CORES)] + [(0, 1)]
 PAIRS = CHIPS // 2
-CHUNKS = 2
+CHUNKS = 1
 GROUP = PAIRS // CHUNKS
+BATCH = 4
 LOADS = [n + PAIRS * part for n in range(PAIRS) for part in range(2)]
 F32 = jnp.float32
 BF16 = jnp.bfloat16
@@ -65,17 +66,19 @@
     return (1 - 2 * (value & 1)).astype(F32)
 
 
+def spread_lane(value, lane):
+    return jnp.broadcast_to(value[:, lane : lane + 1], value.shape)
+
+
 def inverse_factor(held):
     lane = lax.broadcasted_iota(jnp.int32, (BLOCK, ROWS), 1)
     sub = lax.broadcasted_iota(jnp.int32, (BLOCK, ROWS), 0)
+    rows = [jnp.broadcast_to(held[i : i + 1, :], (BLOCK, ROWS)) for i in range(BLOCK)]
     for base in range(0, ROWS, BLOCK):
-        rows = [
-            jnp.broadcast_to(held[base + i : base + i + 1, :], (BLOCK, ROWS)) for i in range(BLOCK)
-        ]
         cell = {}
         for i in range(BLOCK):
             for j in range(i + 1):
-                cell[i, j] = jnp.broadcast_to(rows[i][:, base + j : base + j + 1], (BLOCK, ROWS))
+                cell[i, j] = spread_lane(rows[i], base + j)
         own = jnp.logical_and(lane >= base, lane < base + BLOCK)
         rows = [
             jnp.where(own, jnp.where(lane == base + i, F32(1), F32(0)), rows[i])
@@ -94,12 +97,24 @@
         for i in range(1, BLOCK):
             tile = jnp.where(sub == i, rows[i], tile)
         held[base : base + BLOCK, :] = tile
-        if base + BLOCK < ROWS:
+        after = base + BLOCK
+        if after == ROWS:
+            break
+        coming = []
+        for i in range(BLOCK):
+            row = jnp.broadcast_to(held[after + i : after + i + 1, :], (BLOCK, ROWS))
+            terms = [spread_lane(rows[k], after + i) * rows[k] for k in range(BLOCK)]
+            while len(terms) > 1:
+                terms = [terms[n] + terms[n + 1] for n in range(0, len(terms), 2)]
+            coming.append(jnp.where(own, F32(0), row) - terms[0])
+        rows = coming
+        after = after + BLOCK
+        if after < ROWS:
             update = exact_dot(tile, tile, ((0,), (0,)))
-            rest = held[base + BLOCK :, :]
+            rest = held[after:, :]
             clear = lax.broadcasted_iota(jnp.int32, rest.shape, 1)
             clear = jnp.logical_and(clear >= base, clear < base + BLOCK)
-            held[base + BLOCK :, :] = jnp.where(clear, F32(0), rest) - update[base + BLOCK :, :]
+            held[after:, :] = jnp.where(clear, F32(0), rest) - update[after:, :]
 
 
 def kernel(
@@ -178,35 +193,40 @@
             device_id_type=MESH,
         )
 
-    for chunk in range(CHUNKS):
-        start = chunk * GROUP
-        for step in LOADS[2 * start : 2 * (start + GROUP)]:
-            load(step).wait()
-        both = jnp.concatenate(
-            [slabs[start : start + GROUP], slabs[PAIRS + start : PAIRS + start + GROUP]], axis=0
-        ).reshape(GROUP * HALF, LENGTH)
-        highs, lows = [], []
-        for tile in range(LENGTH // HALF):
-            signs = signs3[tile : tile + 1, :].astype(F32)
-            high, low = split_two(both[:, tile * HALF : (tile + 1) * HALF] * signs)
-            highs.append(high)
-            lows.append(low)
-        left = jnp.concatenate(
-            [jnp.concatenate(highs, axis=1), jnp.concatenate(lows, axis=1)], axis=0
-        )
-        first = jnp.dot(left, table3[...], preferred_element_type=F32)
-        first = first[: GROUP * HALF] + first[GROUP * HALF :]
-        first = first.reshape(2, GROUP, WIDTH, RANK)
-        for pair in range(GROUP):
-            for half in range(CORES):
-                turned = first[:, pair, :, half * HALF : (half + 1) * HALF].reshape(HALF, HALF).T
-                outgoing[half * CHIPS : (half + 1) * CHIPS, start + pair] = turned.reshape(
-                    CHIPS, BLOCK, HALF
-                )
-        if chunk == 0:
-            pl.semaphore_wait(barrier, len(PLANE_STEPS) + len(PLACE_STEPS) - 1)
-        for step in range(len(PLANE_STEPS)):
-            piece(chunk, step).start()
+    left = None
+    for start in range(0, PAIRS + BATCH, BATCH):
+        if start < PAIRS:
+            for step in LOADS[2 * start : 2 * (start + BATCH)]:
+                load(step).wait()
+        if start > 0:
+            first = jnp.dot(left, table3[...], preferred_element_type=F32)
+            first = first[: BATCH * HALF] + first[BATCH * HALF :]
+            first = first.reshape(2, BATCH, WIDTH, RANK)
+            for n in range(BATCH):
+                for half in range(CORES):
+                    turned = first[:, n, :, half * HALF : (half + 1) * HALF]
+                    outgoing[half * CHIPS : (half + 1) * CHIPS, start - BATCH + n] = (
+                        turned.reshape(HALF, HALF).T.reshape(CHIPS, BLOCK, HALF)
+                    )
+        if start < PAIRS:
+            both = jnp.concatenate(
+                [slabs[start : start + BATCH], slabs[PAIRS + start : PAIRS + start + BATCH]],
+                axis=0,
+            ).reshape(BATCH * HALF, LENGTH)
+            highs, lows = [], []
+            for tile in range(LENGTH // HALF):
+                signs = signs3[tile : tile + 1, :].astype(F32)
+                high, low = split_two(both[:, tile * HALF : (tile + 1) * HALF] * signs)
+                highs.append(high)
+                lows.append(low)
+            left = jnp.concatenate(
+                [jnp.concatenate(highs, axis=1), jnp.concatenate(lows, axis=1)], axis=0
+            )
+        if start > 0 and start % GROUP == 0:
+            if start == GROUP:
+                pl.semaphore_wait(barrier, len(PLANE_STEPS) + len(PLACE_STEPS) - 1)
+            for step in range(len(PLANE_STEPS)):
+                piece(start // GROUP - 1, step).start()
 
     landed[p] = outgoing[p]
 

time: 62.9 us -> 61.2 us (0.973)
  Pallas kernels: 61 us -> 59.4 us
    pallas_call x1, Pallas kernels: 61 us -> 59.4 us  [on_device(): pl.pallas_call(kernel, out_shape=jax.ShapeDtypeStruct((RANK // COLS, CHIP...]
where the time goes in v4:
time: 61.2 us; the launch traced here: 61 us
  Pallas kernels  59.4 us (97%)
  local copies, waits for them, and re-layouts  1.57 us (3%)
    pallas_call x1, Pallas kernels, on_device(): pl.pallas_call(kernel, out_shape=jax.ShapeDtypeStruct((RANK // COLS, CHIP...  59.4 us
    unnamed x1, local copies, waits for them, and re-layouts  1.57 us

profile of v4, /device:TPU:1, one launch (start us, length us, event | category | flops | bytes accessed | tf_op | source)
XLA Modules:
  0.0 61.0 jit_solution(11676544930897170233)
XLA Ops:
  0.0 59.4 %sketch_basis.1 = f32[8,16,256]{2,1,0:T(8,128)} custom-call(f32[16,64,2048]{2,1,0:T(8,128)} %tensor.1, s32[16,128]{1,0:T(8,128)} %bitcast.4, s32[2,128]{1,0:T(2,128)} %bitcast.6, s32[16,128]{1,0:T(8,128)} %bitcast.5, s32[2,128]{1,0:T(2,128)} %bitcast.7), custom_call_target="tpu_custom_call" | custom-call | tf_op jit(solution)/shard_map/sketch_basis/pallas_call | solution.py:546
  59.4 1.6 %copy.7 = f32[8,16,256]{2,1,0:T(8,128)} copy(f32[8,16,256]{2,1,0:T(8,128)} %sketch_basis.1) | data formatting | bytes 262144

commit v5 on v4

--- a/solution.py
+++ b/solution.py
@@ -22,13 +22,13 @@
     key=lambda turn: -sum(min(step, SIDE - step) for step in turn),
 )
 CHIP_STEPS = TURNS[:-1]
-PLANE_STEPS = [(dx, dy, dc) for dx, dy in TURNS for dc in (1, 0)][:-1]
+PLANE_STEPS = [(dx, dy, dc) for dc in (1, 0) for dx, dy in TURNS][:-1]
 SLAB_STEPS = [4, 3, 5, 2, 6, 1, 7]
 PLACE_STEPS = [(dz, dc) for dz in SLAB_STEPS for dc in range(CORES)] + [(0, 1)]
 PAIRS = CHIPS // 2
 CHUNKS = 1
 GROUP = PAIRS // CHUNKS
-BATCH = 4
+BATCH = 8
 LOADS = [n + PAIRS * part for n in range(PAIRS) for part in range(2)]
 F32 = jnp.float32
 BF16 = jnp.bfloat16
@@ -120,7 +120,7 @@
 def kernel(
     tensor, signs3_in, picked3_in, signs2_in, picked2_in, out,
     signs3, picked3, signs2, picked2, slabs, table3, table2, outgoing, landed, sketch, slices, planes,
-    columns, spread, row_slices, row_planes, partial_gram, terms, row_block, blocks, block, gram, result,
+    columns, spread, row_slices, row_planes, partial_gram, terms, row_block, blocks, block, gram, row_parts, result,
     small_sem, load_sem, send_sem, recv_sem, slice_send, slice_recv, spread_send, spread_recv, row_send, row_recv,
     term_send, term_recv, block_send, block_recv, gram_send, gram_recv, back_send, back_recv,
 ):
@@ -478,6 +478,11 @@
 
     gram[pl.ds(pl.multiple_of(q * BLOCK, BLOCK), BLOCK), :] = block[...]
 
+    for step in range(len(SLAB_STEPS)):
+        row_slice_arrival(step).wait_recv()
+    row_high, row_low = split_two(row_planes[...].reshape(ROWS, RANK))
+    row_parts[...] = jnp.concatenate([row_high, row_low, row_high], axis=0)
+
     for step in range(len(CHIP_STEPS)):
         gram_arrival(step).wait_recv()
 
@@ -486,10 +491,10 @@
     row = lax.broadcasted_iota(jnp.int32, (ROWS, ROWS), 0)
     col = lax.broadcasted_iota(jnp.int32, (ROWS, ROWS), 1)
     inverse = jnp.where(col <= row, gram[...], F32(0)) * F32(RANK)
-    for step in range(len(SLAB_STEPS)):
-        row_slice_arrival(step).wait_recv()
-    rows = row_planes[...].reshape(ROWS, RANK)
-    result[...] = exact_dot(inverse, rows, ((1,), (0,))).reshape(SLABS, CHIPS, RANK)
+    high, low = split_two(inverse)
+    result[...] = jnp.dot(
+        jnp.concatenate([high, high, low], axis=1), row_parts[...], preferred_element_type=F32
+    ).reshape(SLABS, CHIPS, RANK)
 
     def back_copy(step):
         to = slab_at(SLAB_STEPS[step])
@@ -571,6 +576,7 @@
             pltpu.VMEM((places, BLOCK, ROWS), F32),
             pltpu.VMEM((BLOCK, ROWS), F32),
             pltpu.VMEM((ROWS, ROWS), F32),
+            pltpu.VMEM((3 * ROWS, RANK), BF16),
             pltpu.VMEM((SLABS, CHIPS, RANK), F32),
             dma((4,)),
             dma((CHIPS,)),

time: 61.2 us -> 61 us (level)
  no operation moved by 1% of the time
where the time goes in v5:
time: 61 us; the launch traced here: 60.9 us
  Pallas kernels  59.3 us (97%)
  local copies, waits for them, and re-layouts  1.57 us (3%)
    pallas_call x1, Pallas kernels, on_device(): pl.pallas_call(kernel, out_shape=jax.ShapeDtypeStruct((RANK // COLS, CHIP...  59.3 us
    unnamed x1, local copies, waits for them, and re-layouts  1.57 us

profile of v5, /device:TPU:1, one launch (start us, length us, event | category | flops | bytes accessed | tf_op | source)
XLA Modules:
  0.0 60.9 jit_solution(16163279541039429684)
XLA Ops:
  0.0 59.3 %sketch_basis.1 = f32[8,16,256]{2,1,0:T(8,128)} custom-call(f32[16,64,2048]{2,1,0:T(8,128)} %tensor.1, s32[16,128]{1,0:T(8,128)} %bitcast.4, s32[2,128]{1,0:T(2,128)} %bitcast.6, s32[16,128]{1,0:T(8,128)} %bitcast.5, s32[2,128]{1,0:T(2,128)} %bitcast.7), custom_call_target="tpu_custom_call" | custom-call | tf_op jit(solution)/shard_map/sketch_basis/pallas_call | solution.py:551
  59.3 1.6 %copy.7 = f32[8,16,256]{2,1,0:T(8,128)} copy(f32[8,16,256]{2,1,0:T(8,128)} %sketch_basis.1) | data formatting | bytes 262144
